TPU v7x, 32 devices: a whole 2x2x4 slice. The times are simulated.
32 devices in a mesh: space: 8 (over z, y), chan: 4 (over x, core).
Axes of the slice: x: 2, y: 2, z: 4, core: 2. Of those that a mesh axis runs over, the one named last changes fastest.
Arguments:
- latents: bfloat16 [64, 2, 640, 128], P('space', None, 'chan'), as said below
- targets: bfloat16 [64, 2, 640, 128], P('space', None, 'chan'), may hold values from -6 to 6
- norm_gain: float32 [640], P('chan'), may hold values from 0.5 to 2
- norm_bias: float32 [640], P('chan'), may hold values from -2.5 to 2.5
- conv_weight: bfloat16 [3, 3, 640, 640], P(None, None, 'chan'), may hold values from -0.078125 to 0.078125
- tile_image: int32 [8, 8], replicated, may hold values from -1 to 15, as said below
- tile_owner: int32 [8, 8], replicated, may hold values from -1 to 7, as said below
- tile_slot: int32 [8, 8], replicated, may hold values from -1 to 3, as said below
- timesteps: int32 [16], replicated, may hold values from 0 to 999
Outputs:
- x_grad: bfloat16 [32, 2, 640, 128], P('space', None, 'chan')
- weight_grad: float32 [3, 3, 640, 640], P(None, None, 'chan')
Inputs may be any that keep to these rules, and one draw needn't show every extreme that they name: `tile_image`: every index s of space holds the tiles of exactly two images, each in consecutive slots in row order from the image's first row; unused slots come last and hold -1. Every image has one tile or more, all indices together hold 32 tiles, and some index has all 8 slots used. `tile_owner`: for a used slot, the index along space that computes the tile; -1 for unused slots. Every index receives exactly 4 tiles, and no index sends more than 1 tile to one index, a bound that some pair reaches. `tile_slot`: for a used slot, the tile's position among the 4 tiles of its assigned index, each position taken once; -1 for unused slots. `latents`: latent features of the images.
All inputs are finite; a program needn't handle non-finite values.
Results may differ from a plain program's by a relative error of at most 0.018.
Values may be sent and summed in bfloat16 or wider, within the bound.
A program may use at most 128 MiB of HBM per device.

v0:
```python
import math

import jax
import jax.numpy as jnp
from jax import lax
from jax.sharding import PartitionSpec as P

GROUPS = 32


EPS = 1e-05
HIGH = lax.Precision.HIGHEST


def loss_weights(timesteps):
    phase = (timesteps.astype(jnp.float32) / 1000.0 + 0.008) / 1.008 * (math.pi / 2.0)
    alpha_bar = jnp.cos(phase) ** 2
    return jnp.minimum(1.0, 5.0 * (1.0 - alpha_bar) / alpha_bar)


def silu_slope(pre_act):
    sigma_val = jax.nn.sigmoid(pre_act)
    return sigma_val * (1.0 + pre_act * (1.0 - sigma_val))


def group_sums(values, groups):
    grouped = values.reshape(
        values.shape[:-2] + (groups, values.shape[-2] // groups, values.shape[-1])
    )
    return jnp.sum(grouped, axis=(-2, -1))


def norm_stats(sum_first, sum_second, counts):
    mean_img = sum_first / counts[:, None]
    var_img = sum_second / counts[:, None] - mean_img * mean_img
    return (mean_img, lax.rsqrt(var_img + EPS))


def conv_views(row_views, weight):
    running = None
    for row_tap in range(3):
        source = row_views[row_tap]
        col_count = source.shape[-1]
        padded = jnp.pad(source, ((0, 0), (0, 0), (0, 0), (1, 1)))
        for col_tap in range(3):
            window = padded[:, :, :, col_tap : col_tap + col_count]
            tap_term = jnp.einsum(
                "nrcw,oc->nrow",
                window,
                weight[row_tap, col_tap],
                preferred_element_type=jnp.float32,
            )
            running = tap_term if running is None else running + tap_term
    return running


def weight_terms(row_views, grad_field):
    tap_rows = []
    for row_tap in range(3):
        source = row_views[row_tap]
        col_count = source.shape[-1]
        padded = jnp.pad(source, ((0, 0), (0, 0), (0, 0), (1, 1)))
        tap_cols = []
        for col_tap in range(3):
            window = padded[:, :, :, col_tap : col_tap + col_count]
            tap_cols.append(
                jnp.einsum("nrow,nrcw->oc", grad_field, window, preferred_element_type=jnp.float32)
            )
        tap_rows.append(jnp.stack(tap_cols))
    return jnp.stack(tap_rows)


def owner_rank(owners):
    slot_count = owners.shape[-1]
    earlier = jnp.arange(slot_count)[None, :] < jnp.arange(slot_count)[:, None]
    same_owner = owners[..., :, None] == owners[..., None, :]
    return jnp.sum(same_owner & earlier, axis=-1)


def sender_table(my_owner, devices, capacity):
    column_of = my_owner * capacity + owner_rank(my_owner)
    column_ids = jnp.arange(devices * capacity, dtype=jnp.int32)
    return ((column_of[None, :] == column_ids[:, None]) & (my_owner[None, :] >= 0)).astype(
        jnp.bfloat16
    )


def receiver_table(tile_owner, tile_slot, my_index, tiles_dev, capacity):
    devices = tile_owner.shape[0]
    column_of = jnp.arange(devices, dtype=jnp.int32)[:, None] * capacity + owner_rank(tile_owner)
    slot_ids = jnp.arange(tiles_dev, dtype=jnp.int32)
    hit_mask = (tile_owner[None] == my_index) & (tile_slot[None] == slot_ids[:, None, None])
    column_ids = jnp.arange(devices * capacity, dtype=jnp.int32)
    table = jnp.sum(
        (hit_mask[..., None] & (column_of[None, :, :, None] == column_ids)).astype(jnp.float32),
        axis=(1, 2),
    )
    return (table.astype(jnp.bfloat16), hit_mask)


def gather_channels(act):
    return lax.all_gather(act, "chan", axis=2, tiled=True)


def sum_channels(partial_grad):
    return lax.psum_scatter(
        partial_grad.astype(jnp.bfloat16), "chan", scatter_dimension=2, tiled=True
    ).astype(jnp.float32)


def receive_tiles(outgoing):
    return lax.all_to_all(outgoing, "space", split_axis=0, concat_axis=0, tiled=True)


def local(
    latents,
    targets,
    norm_gain,
    norm_bias,
    conv_weight,
    tile_image,
    tile_owner,
    tile_slot,
    timesteps,
):
    my_index = lax.axis_index("space")
    devices = lax.axis_size("space")
    slots_dev, tile_rows, local_ch, col_count = latents.shape
    channels = conv_weight.shape[3]
    group_size = channels // GROUPS
    groups_here = local_ch // group_size
    image_total = timesteps.shape[0]
    tiles_dev = slots_dev // 2
    capacity = -(-slots_dev // devices)
    image_ids = jnp.arange(image_total, dtype=jnp.int32)
    counts = jnp.sum(
        (tile_image.reshape(-1)[None, :] == image_ids[:, None]).astype(jnp.float32), axis=1
    ) * float(tile_rows * col_count * group_size)
    weights_img = loss_weights(timesteps)
    flipped = jnp.transpose(conv_weight[::-1, ::-1], (0, 1, 3, 2))
    gain_col = norm_gain[:, None]
    bias_col = norm_bias[:, None]
    grad_scale = 1.0 / math.sqrt(devices * tiles_dev * tile_rows * col_count)
    my_image = lax.dynamic_index_in_dim(tile_image, my_index, 0, keepdims=False)
    my_owner = lax.dynamic_index_in_dim(tile_owner, my_index, 0, keepdims=False)
    send_table = sender_table(my_owner, devices, capacity)
    recv_table, hit_mask = receiver_table(tile_owner, tile_slot, my_index, tiles_dev, capacity)
    prev_local = jnp.concatenate([jnp.full((1,), -2, jnp.int32), my_image[:-1]])
    next_local = jnp.concatenate([my_image[1:], jnp.full((1,), -2, jnp.int32)])
    up_slot = ((prev_local == my_image) & (my_image >= 0)).astype(jnp.bfloat16)[:, None, None, None]
    down_slot = ((next_local == my_image) & (my_image >= 0)).astype(jnp.bfloat16)[
        :, None, None, None
    ]

    def with_rims(source_field):
        zero_tile = jnp.zeros_like(source_field[:1])
        rows_above = jnp.concatenate([zero_tile, source_field[:-1]], axis=0) * up_slot
        rows_below = jnp.concatenate([source_field[1:], zero_tile], axis=0) * down_slot
        return jnp.concatenate([rows_above, source_field, rows_below], axis=1)

    packed = jnp.stack([with_rims(latents), with_rims(targets)], axis=1)
    outgoing = jnp.dot(
        send_table, packed.reshape(slots_dev, -1), preferred_element_type=jnp.float32
    ).astype(jnp.bfloat16)
    outgoing = outgoing.reshape(devices, capacity, -1)
    prev_all = jnp.concatenate([jnp.full((devices, 1), -2, jnp.int32), tile_image[:, :-1]], axis=1)
    next_all = jnp.concatenate([tile_image[:, 1:], jnp.full((devices, 1), -2, jnp.int32)], axis=1)
    tile_img = jnp.sum(jnp.where(hit_mask, tile_image[None], 0), axis=(1, 2))
    prev_img = jnp.sum(jnp.where(hit_mask, prev_all[None], 0), axis=(1, 2))
    next_img = jnp.sum(jnp.where(hit_mask, next_all[None], 0), axis=(1, 2))
    onehot_tiles = (tile_img[:, None] == image_ids[None, :]).astype(jnp.float32)
    placed = jnp.dot(
        recv_table,
        receive_tiles(outgoing).reshape(devices * capacity, -1),
        preferred_element_type=jnp.float32,
    ).astype(jnp.bfloat16)
    tiles = placed.reshape(tiles_dev, 2, tile_rows + 4, local_ch, col_count)
    core_float = tiles[:, 0, 2 : 2 + tile_rows].astype(jnp.float32)
    part_first = jnp.dot(
        onehot_tiles.T, jnp.sum(group_sums(core_float, groups_here), axis=1), precision=HIGH
    )
    part_second = jnp.dot(
        onehot_tiles.T,
        jnp.sum(group_sums(core_float * core_float, groups_here), axis=1),
        precision=HIGH,
    )
    sum_first, sum_second = lax.psum((part_first, part_second), "space")
    mean_img, rstd_img = norm_stats(sum_first, sum_second, counts)
    mean_tile = jnp.repeat(jnp.dot(onehot_tiles, mean_img, precision=HIGH), group_size, axis=1)[
        :, None, :, None
    ]
    rstd_tile = jnp.repeat(jnp.dot(onehot_tiles, rstd_img, precision=HIGH), group_size, axis=1)[
        :, None, :, None
    ]
    prev_ok = (prev_img == tile_img).astype(jnp.float32)[:, None]
    next_ok = (next_img == tile_img).astype(jnp.float32)[:, None]
    row_ok = jnp.concatenate(
        [
            jnp.repeat(prev_ok, 2, axis=1),
            jnp.ones((tiles_dev, tile_rows), jnp.float32),
            jnp.repeat(next_ok, 2, axis=1),
        ],
        axis=1,
    )
    lat_tile = tiles[:, 0].astype(jnp.float32)
    normed = (lat_tile - mean_tile) * rstd_tile
    pre_act = normed * gain_col + bias_col
    act = (jax.nn.silu(pre_act) * row_ok[:, :, None, None]).astype(jnp.bfloat16)
    act_full = gather_channels(act)
    prediction = conv_views(
        [act_full[:, : tile_rows + 2], act_full[:, 1 : tile_rows + 3], act_full[:, 2:]], conv_weight
    )
    loss_tile = jnp.dot(onehot_tiles, weights_img, precision=HIGH)[:, None, None, None]
    target_float = tiles[:, 1, 1 : tile_rows + 3].astype(jnp.float32)
    out_grad = (
        loss_tile * (prediction - target_float) * row_ok[:, 1 : tile_rows + 3, None, None]
    ).astype(jnp.bfloat16)
    act_grad = sum_channels(
        conv_views(
            [out_grad[:, :tile_rows], out_grad[:, 1 : tile_rows + 1], out_grad[:, 2:]], flipped
        )
    )
    core_normed = normed[:, 2 : 2 + tile_rows]
    norm_grad = act_grad * silu_slope(pre_act[:, 2 : 2 + tile_rows]) * gain_col
    grad_first = jnp.dot(
        onehot_tiles.T, jnp.sum(group_sums(norm_grad, groups_here), axis=1), precision=HIGH
    )
    grad_second = jnp.dot(
        onehot_tiles.T,
        jnp.sum(group_sums(norm_grad * core_normed, groups_here), axis=1),
        precision=HIGH,
    )
    grad_first, grad_second = lax.psum((grad_first, grad_second), "space")
    mean_g = jnp.repeat(
        jnp.dot(onehot_tiles, grad_first / counts[:, None], precision=HIGH), group_size, axis=1
    )[:, None, :, None]
    mean_gn = jnp.repeat(
        jnp.dot(onehot_tiles, grad_second / counts[:, None], precision=HIGH), group_size, axis=1
    )[:, None, :, None]
    x_grad = (rstd_tile * (norm_grad - mean_g - core_normed * mean_gn)).astype(jnp.bfloat16)
    weight_sum = weight_terms(
        [
            act_full[:, 1 : tile_rows + 1],
            act_full[:, 2 : tile_rows + 2],
            act_full[:, 3 : tile_rows + 3],
        ],
        out_grad[:, 1 : tile_rows + 1],
    )
    weight_grad = lax.psum((weight_sum * grad_scale).astype(jnp.bfloat16), "space").astype(
        jnp.float32
    )
    return (x_grad, weight_grad)


def solution(mesh):
    in_specs = (
        P("space", None, "chan", None),
        P("space", None, "chan", None),
        P("chan"),
        P("chan"),
        P(None, None, "chan", None),
        P(),
        P(),
        P(),
        P(),
    )
    out_specs = (P("space", None, "chan", None), P(None, None, "chan", None))
    return jax.shard_map(local, mesh=mesh, in_specs=in_specs, out_specs=out_specs, check_vma=False)
```

profile of v0, /device:TPU:0, one launch (start us, length us, event | category | flops | bytes accessed | tf_op | source)
XLA Modules:
  0.0 389.4 jit_solution(16042484266506255146)
XLA Ops:
  10.3 1.3 fusion.155
  14.1 4.3 %fusion = bf16[8,1,245760]{2,0,1:T(8,128)(2,1)} fusion(bf16[1,8,1920,128]{3,2,1,0:T(8,128)(2,1)S(1)} %bitcast.277, s32[8]{0:T(128)S(1)} %fusion.106, pred[8]{0:T(512)(128)(4,1)S(1)} %compare_bitcast_fusion), kind=kOutput, calls=%fused_computation.1 | convolution fusion | flops 33423488 | bytes 7864360 | tf_op jit(solution)/shard_map/dot_general | solution.py:162
  18.9 6.0 %reduce.12 = bf16[8,245760]{1,0:T(8,128)(2,1)} reduce(bf16[8,1,245760]{2,0,1:T(8,128)(2,1)} %fusion, bf16[]{:T(256)} %broadcast.154), dimensions={1}, to_apply=%copy.61.reduce_sub_computation | reduce | bytes 7864322 | tf_op jit(solution)/shard_map/reshape | solution.py:165
  24.9 7.7 %reshape.180 = bf16[8,2,122880]{2,1,0:T(2,128)(2,1)} reshape(bf16[8,245760]{1,0:T(8,128)(2,1)} %reduce.12) | data formatting | bytes 7864320
  32.6 7.4 %all-to-all-start = ((bf16[8,2,122880]{2,1,0:T(2,128)(2,1)}), bf16[8,2,122880]{2,1,0:T(2,128)(2,1)}, u32[]{:S(2)}, u32[]{:S(2)}) async-start(bf16[8,2,122880]{2,1,0:T(2,128)(2,1)} %reshape.180), calls=%async_computation | async-start | bytes 7864320 | tf_op jit(solution)/shard_map/all_to_all | solution.py:112
  41.7 85.9 %all-to-all-done = bf16[8,2,122880]{2,1,0:T(2,128)(2,1)} async-done(((bf16[8,2,122880]{2,1,0:T(2,128)(2,1)}), bf16[8,2,122880]{2,1,0:T(2,128)(2,1)}, u32[]{:S(2)}, u32[]{:S(2)}) %all-to-all-start) | async-done | bytes 3932192 | tf_op jit(solution)/shard_map/all_to_all | solution.py:112
  127.7 8.5 %reshape.181 = bf16[8,1,245760]{2,1,0:T(2,128)(2,1)} reshape(bf16[8,2,122880]{2,1,0:T(2,128)(2,1)} %all-to-all-done) | data formatting | bytes 7864320
  136.2 7.8 %fusion.13 = bf16[1,4,1920,128]{3,1,2,0:T(4,128)(2,1)S(1)} fusion(bf16[8,1,245760]{2,1,0:T(2,128)(2,1)} %reshape.181, bf16[4,8]{1,0:T(4,128)(2,1)S(1)} %convert_reduce_fusion.1), kind=kOutput, calls=%fused_computation.36 | convolution fusion | flops 16711680 | bytes 5898304 | tf_op jit(solution)/shard_map/dot_general | solution.py:172
  144.3 1.3 copy-done.5
  146.7 19.8 %all-reduce.16 = (f32[16,8]{0,1:T(8,128)S(1)}, f32[16,8]{0,1:T(8,128)S(1)}) all-reduce(f32[16,8]{0,1:T(8,128)S(1)} %fusion.94, f32[16,8]{0,1:T(8,128)S(1)} %fusion.93), channel_id=1, replica_groups=mesh['space'=8,'chan'=4] {'space'}, use_global_device_ids=true, to_apply=%region_6.7 | all-reduce | flops 256 | bytes 2048 | tf_op jit(solution)/shard_map/psum | solution.py:187
  167.2 4.5 %multiply_convert_fusion = (bf16[4,6,160,128]{3,2,1,0:T(8,128)(2,1)}, f32[4,6,160,128]{3,2,1,0:T(8,128)}, f32[4,6,160,128]{3,2,1,0:T(8,128)}) fusion(f32[4,6]{1,0:T(4,128)S(1)} %pad_maximum_fusion.1, f32[160]{0:T(256)S(1)} %copy-done.15, f32[160]{0:T(256)S(1)} %copy-done.13, f32[4,160]{1,0:T(4,128)S(1)} %mul.150, f32[4,160]{1,0:T(4,128)S(1)} %sub.37, ...), kind=kLoop, calls=%fused_computation.33 | loop fusion | flops 5406720 | bytes 5904736 | tf_op jit(solution)/shard_map/convert_element_type | solution.py:208
  172.0 1.4 reverse_bitcast_fusion
  173.5 28.7 %all-gather.2.cloned.1.call-done = bf16[4,6,640,128]{3,2,1,0:T(8,128)(2,1)} async-done(((bf16[4,6,160,128]{3,2,1,0:T(8,128)(2,1)}), bf16[4,6,640,128]{3,2,1,0:T(8,128)(2,1)}) %all-gather.2.cloned.1.call-update) | async-done | bytes 3932176 | tf_op jit(solution)/shard_map/all_gather | solution.py:102
  202.2 2.6 fusion.60
  205.1 1.0 fusion.153
  207.0 1.0 fusion.25
  208.8 1.0 fusion.24
  211.5 1.0 fusion.21
  212.5 2.2 fusion.29
  220.4 1.5 fusion.44
  222.0 3.0 fusion.43
  225.0 3.0 fusion.48
  230.2 1.7 fusion.5
  232.0 1.8 fusion.46
  237.2 1.3 copy-done.1
  238.5 2.9 fusion.28
  241.4 86.5 %all-reduce.19.cloned.1.call-done = bf16[3,3,160,640]{3,2,1,0:T(8,128)(2,1)} async-done(((bf16[3,3,160,640]{3,2,1,0:T(8,128)(2,1)}), bf16[3,3,160,640]{3,2,1,0:T(8,128)(2,1)}) %all-reduce.19.cloned.1.call-update) | async-done | bytes 1843216 | tf_op jit(solution)/shard_map/psum | solution.py:249
  327.9 3.6 convert_element_type.121
  331.5 25.1 %reduce-scatter.2.cloned.1.call-done = bf16[4,2,160,128]{3,2,1,0:T(8,128)(2,1)} async-done(((bf16[4,2,640,128]{3,2,1,0:T(8,128)(2,1)}), bf16[4,2,160,128]{3,2,1,0:T(8,128)(2,1)}) %reduce-scatter.2.cloned.1.call-update) | async-done | bytes 327696 | tf_op jit(solution)/shard_map/reduce_scatter | solution.py:106
  356.6 1.7 fusion.150
  359.0 21.6 %all-reduce.15 = (f32[16,8]{0,1:T(8,128)S(1)}, f32[16,8]{0,1:T(8,128)S(1)}) all-reduce(f32[16,8]{0,1:T(8,128)S(1)} %fusion.90, f32[16,8]{0,1:T(8,128)S(1)} %fusion.91), channel_id=1, replica_groups=mesh['space'=8,'chan'=4] {'space'}, use_global_device_ids=true, to_apply=%region_19.20 | all-reduce | flops 256 | bytes 2048 | tf_op jit(solution)/shard_map/psum | solution.py:233
  381.3 1.1 multiply_convert_fusion.1
  (121 shorter events, 26.4 us)
Async XLA Ops:
  7.2 4.4 %copy-start.8 = (bf16[8,2,160,128]{3,2,1,0:T(8,128)(2,1)S(1)}, bf16[8,2,160,128]{3,2,1,0:T(8,128)(2,1)}, u32[]{:S(2)}) copy-start(bf16[8,2,160,128]{3,2,1,0:T(8,128)(2,1)} %param.10) | copy-start | bytes 1966084
  10.3 1.5 copy-start.11
  11.9 1.1 copy-start.7
  32.6 8.1 %copy-start.12 = (s32[8,8]{1,0:T(8,128)S(1)}, s32[8,8]{1,0:T(8,128)}, u32[]{:S(2)}) copy-start(s32[8,8]{1,0:T(8,128)} %param.15) | copy-start | bytes 772
  32.6 8.5 %copy-start.14 = (s32[8,8]{1,0:T(8,128)S(1)}, s32[8,8]{1,0:T(8,128)}, u32[]{:S(2)}) copy-start(s32[8,8]{1,0:T(8,128)} %param.16) | copy-start | bytes 772
  32.6 95.1 %all-to-all-start = ((bf16[8,2,122880]{2,1,0:T(2,128)(2,1)}), bf16[8,2,122880]{2,1,0:T(2,128)(2,1)}, u32[]{:S(2)}, u32[]{:S(2)}) async-start(bf16[8,2,122880]{2,1,0:T(2,128)(2,1)} %reshape.180), calls=%async_computation | async-start | bytes 7864320 | tf_op jit(solution)/shard_map/all_to_all | solution.py:112
  40.0 162.2 %all-gather.2.cloned.1.call-start = ((), (), s32[]{:S(2)}) async-start(), calls=%async_computation.2 | async-start | bytes 4915200 | tf_op jit(solution)/shard_map/all_gather | solution.py:102
  144.0 23.1 %copy-start.13 = (f32[160]{0:T(256)S(1)}, f32[160]{0:T(256)}, u32[]{:S(2)}) copy-start(f32[160]{0:T(256)} %param.11) | copy-start | bytes 1924
  144.0 23.1 %copy-start.15 = (f32[160]{0:T(256)S(1)}, f32[160]{0:T(256)}, u32[]{:S(2)}) copy-start(f32[160]{0:T(256)} %param.12) | copy-start | bytes 1924
  144.3 1.3 copy-start.5
  167.2 4.7 %copy-start.16 = (s32[16]{0:T(128)S(1)}, s32[16]{0:T(128)}, u32[]{:S(2)}) copy-start(s32[16]{0:T(128)} %param.17) | copy-start | bytes 196
  167.2 4.9 %copy-start.4 = (bf16[3,3,160,640]{3,2,1,0:T(8,128)(2,1)S(1)}, bf16[3,3,160,640]{3,2,1,0:T(8,128)(2,1)}, u32[]{:S(2)}) copy-start(bf16[3,3,160,640]{3,2,1,0:T(8,128)(2,1)} %param.13) | copy-start | bytes 5529604
  171.7 156.1 %all-reduce.19.cloned.1.call-start = ((), (), s32[]{:S(2)}) async-start(), calls=%async_computation.4 | async-start | bytes 3686400 | tf_op jit(solution)/shard_map/psum | solution.py:249
  202.1 2.9 copy-start
  231.9 124.7 %reduce-scatter.2.cloned.1.call-start = ((), (), s32[]{:S(2)}) async-start(), calls=%async_computation.3 | async-start | bytes 1638400 | tf_op jit(solution)/shard_map/reduce_scatter | solution.py:106
  232.0 1.8 copy-start.3
  232.0 1.8 copy-start.9
  233.8 1.0 copy-start.10
  235.4 1.7 copy-start.2
  236.0 2.5 copy-start.1
  241.4 115.2 %copy-start.6 = (f32[4,6,160,128]{3,2,1,0:T(8,128)S(1)}, f32[4,6,160,128]{3,2,1,0:T(8,128)}, u32[]{:S(2)}) copy-start(f32[4,6,160,128]{3,2,1,0:T(8,128)} %get-tuple-element.23) | copy-start | bytes 5898244
Sparse Core Ops, SparseCore 0:
  171.9 30.2 all-gather.1
  232.0 95.7 all-reduce.18
  330.4 26.1 reduce-scatter.1
where the time goes:
time: 397 us; the launch traced here: 389 us
  waiting for transfers between devices  226 us (57%)
  matrix products  45.4 us (11%)
  blocking collectives  41.4 us (10%)
  local copies, waits for them, and re-layouts  30.6 us (8%)
  other arithmetic  23.4 us (6%)
  between operations  14.7 us (4%)
  starting transfers between devices  7.71 us (2%)
    psum x1, waiting for transfers between devices, local(): lax.psum((weight_sum * grad_scale).astype(jnp.bfloat16), 'space')  86.5 us
    all_to_all x1, waiting for transfers between devices, receive_tiles(): lax.all_to_all(outgoing, 'space', split_axis=0, concat_axis=0, tiled=True)  85.9 us
    all_gather x1, waiting for transfers between devices, gather_channels(): return lax.all_gather(act, 'chan', axis=2, tiled=True)  28.7 us
    dot_general x18, matrix products, conv_views(): jnp.einsum('nrcw,oc->nrow', window, weight[row_tap, col_tap], preferred_e...  25.7 us
    reduce_scatter x1, waiting for transfers between devices, sum_channels(): lax.psum_scatter(partial_grad.astype(jnp.bfloat16), 'chan', scatter_dimen...  25.1 us
    psum x1, blocking collectives, local(): grad_first, grad_second = lax.psum((grad_first, grad_second), 'space')  21.6 us
    unnamed x37, local copies, waits for them, and re-layouts  21.2 us
    psum x1, blocking collectives, local(): sum_first, sum_second = lax.psum((part_first, part_second), 'space')  19.8 us
  transfers between devices with their start and end apart: 4, of which 4 were waited for; matrix products, arithmetic and copies ran while one was open for 4% of the time, Pallas kernels for 0%

commit v1 on v0

v1 whole, which is shorter than its diff:
```python
import math

import jax
import jax.numpy as jnp
from jax import lax
from jax.sharding import PartitionSpec as P

GROUPS = 32


EPS = 1e-05
HIGH = lax.Precision.HIGHEST


def loss_weights(timesteps):
    phase = (timesteps.astype(jnp.float32) / 1000.0 + 0.008) / 1.008 * (math.pi / 2.0)
    alpha_bar = jnp.cos(phase) ** 2
    return jnp.minimum(1.0, 5.0 * (1.0 - alpha_bar) / alpha_bar)


def silu_slope(pre_act):
    sigma_val = jax.nn.sigmoid(pre_act)
    return sigma_val * (1.0 + pre_act * (1.0 - sigma_val))


def group_sums(values, groups):
    grouped = values.reshape(
        values.shape[:-2] + (groups, values.shape[-2] // groups, values.shape[-1])
    )
    return jnp.sum(grouped, axis=(-2, -1))


def norm_stats(sum_first, sum_second, counts):
    mean_img = sum_first / counts[:, None]
    var_img = sum_second / counts[:, None] - mean_img * mean_img
    return (mean_img, lax.rsqrt(var_img + EPS))


def conv_views(row_views, weight):
    running = None
    for row_tap in range(3):
        source = row_views[row_tap]
        col_count = source.shape[-1]
        padded = jnp.pad(source, ((0, 0), (0, 0), (0, 0), (1, 1)))
        for col_tap in range(3):
            window = padded[:, :, :, col_tap : col_tap + col_count]
            tap_term = jnp.einsum(
                "nrcw,oc->nrow",
                window,
                weight[row_tap, col_tap],
                preferred_element_type=jnp.float32,
            )
            running = tap_term if running is None else running + tap_term
    return running


def weight_terms(row_views, grad_field):
    tap_rows = []
    for row_tap in range(3):
        source = row_views[row_tap]
        col_count = source.shape[-1]
        padded = jnp.pad(source, ((0, 0), (0, 0), (0, 0), (1, 1)))
        tap_cols = []
        for col_tap in range(3):
            window = padded[:, :, :, col_tap : col_tap + col_count]
            tap_cols.append(
                jnp.einsum("nrow,nrcw->oc", grad_field, window, preferred_element_type=jnp.float32)
            )
        tap_rows.append(jnp.stack(tap_cols))
    return jnp.stack(tap_rows)


def gather_channels(act):
    return lax.all_gather(act, "chan", axis=2, tiled=True)


def sum_channels(partial_grad):
    return lax.psum_scatter(
        partial_grad.astype(jnp.bfloat16), "chan", scatter_dimension=2, tiled=True
    ).astype(jnp.float32)


def receive_tiles(outgoing):
    return lax.all_to_all(outgoing, "space", split_axis=0, concat_axis=0, tiled=True)


def local(
    latents,
    targets,
    norm_gain,
    norm_bias,
    conv_weight,
    tile_image,
    tile_owner,
    tile_slot,
    timesteps,
):
    my_index = lax.axis_index("space")
    devices = lax.axis_size("space")
    slots_dev, tile_rows, local_ch, col_count = latents.shape
    channels = conv_weight.shape[3]
    group_size = channels // GROUPS
    groups_here = local_ch // group_size
    image_total = timesteps.shape[0]
    tiles_dev = slots_dev // 2
    image_ids = jnp.arange(image_total, dtype=jnp.int32)
    counts = jnp.sum(
        (tile_image.reshape(-1)[None, :] == image_ids[:, None]).astype(jnp.float32), axis=1
    ) * float(tile_rows * col_count * group_size)
    weights_img = loss_weights(timesteps)
    flipped = jnp.transpose(conv_weight[::-1, ::-1], (0, 1, 3, 2))
    gain_col = norm_gain[:, None]
    bias_col = norm_bias[:, None]
    grad_scale = 1.0 / math.sqrt(devices * tiles_dev * tile_rows * col_count)
    my_image = lax.dynamic_index_in_dim(tile_image, my_index, 0, keepdims=False)
    my_owner = lax.dynamic_index_in_dim(tile_owner, my_index, 0, keepdims=False)
    rows = slots_dev * tile_rows
    row_image = jnp.repeat(my_image, tile_rows)
    valid = row_image >= 0
    edge = jnp.full((1,), -2, jnp.int32)
    up_ok = valid & (jnp.concatenate([edge, row_image[:-1]]) == row_image)
    down_ok = valid & (jnp.concatenate([row_image[1:], edge]) == row_image)
    onehot = (row_image[:, None] == image_ids[None, :]).astype(jnp.float32)

    def shifted(field):
        zero = jnp.zeros_like(field[:, :1])
        above = jnp.concatenate([zero, field[:, :-1]], axis=1)
        below = jnp.concatenate([field[:, 1:], zero], axis=1)
        above = jnp.where(up_ok[None, :, None, None], above, 0)
        below = jnp.where(down_ok[None, :, None, None], below, 0)
        return [above, field, below]

    def per_row(per_image):
        out = jnp.dot(onehot, per_image, precision=HIGH)
        return jnp.repeat(out, group_size, axis=1)[None, :, :, None]

    def per_image(values):
        return jnp.dot(onehot.T, group_sums(values, groups_here)[0], precision=HIGH)

    lat = latents.reshape(1, rows, local_ch, col_count).astype(jnp.float32)
    mean_img, rstd_img = norm_stats(
        per_image(lat), per_image(lat * lat), jnp.maximum(counts, 1.0)
    )
    mean_rows, rstd_rows = per_row(mean_img), per_row(rstd_img)
    valid_rows = valid[None, :, None, None]
    normed = (lat - mean_rows) * rstd_rows
    pre_act = normed * gain_col + bias_col
    act = jnp.where(valid_rows, jax.nn.silu(pre_act), 0.0).astype(jnp.bfloat16)
    views = shifted(gather_channels(act))
    prediction = conv_views(views, conv_weight)
    loss_rows = jnp.dot(onehot, weights_img, precision=HIGH)[None, :, None, None]
    target = targets.reshape(1, rows, local_ch, col_count).astype(jnp.float32)
    out_grad = jnp.where(valid_rows, loss_rows * (prediction - target), 0.0).astype(jnp.bfloat16)
    weight_sum = weight_terms(views, out_grad)
    weight_grad = lax.psum((weight_sum * grad_scale).astype(jnp.bfloat16), "space").astype(
        jnp.float32
    )
    act_grad = sum_channels(conv_views(shifted(out_grad), flipped))
    norm_grad = act_grad * silu_slope(pre_act) * gain_col
    mean_g = per_row(per_image(norm_grad) / jnp.maximum(counts, 1.0)[:, None])
    mean_gn = per_row(per_image(norm_grad * normed) / jnp.maximum(counts, 1.0)[:, None])
    x_grad = (rstd_rows * (norm_grad - mean_g - normed * mean_gn)).astype(jnp.bfloat16)
    x_tiles = x_grad.reshape(latents.shape)
    device_ids = jnp.arange(devices, dtype=jnp.int32)
    from_slot = jnp.argmax(my_owner[None, :] == device_ids[:, None], axis=1)
    outgoing = jnp.stack(
        [lax.dynamic_index_in_dim(x_tiles, from_slot[d], 0, False) for d in range(devices)]
    )
    arrived = receive_tiles(outgoing)
    slot_ids = jnp.arange(tiles_dev, dtype=jnp.int32)
    hits = (tile_owner[None] == my_index) & (tile_slot[None] == slot_ids[:, None, None])
    source = jnp.argmax(jnp.any(hits, axis=2), axis=1)
    x_out = jnp.stack(
        [lax.dynamic_index_in_dim(arrived, source[t], 0, False) for t in range(tiles_dev)]
    )
    return (x_out, weight_grad)


def solution(mesh):
    in_specs = (
        P("space", None, "chan", None),
        P("space", None, "chan", None),
        P("chan"),
        P("chan"),
        P(None, None, "chan", None),
        P(),
        P(),
        P(),
        P(),
    )
    out_specs = (P("space", None, "chan", None), P(None, None, "chan", None))
    return jax.shard_map(local, mesh=mesh, in_specs=in_specs, out_specs=out_specs, check_vma=False)
```

time: 397 us -> 261 us (0.66)
  the two profiles are of different devices: /device:TPU:0 before, /device:TPU:18 now
where the time goes in v1:
time: 261 us; the launch traced here: 258 us
  waiting for transfers between devices  114 us (44%)
  matrix products  64.6 us (25%)
  between operations  37.3 us (14%)
  other arithmetic  18.6 us (7%)
  local copies, waits for them, and re-layouts  17.6 us (7%)
  starting transfers between devices  6.16 us (2%)
    psum x1, waiting for transfers between devices, local(): lax.psum((weight_sum * grad_scale).astype(jnp.bfloat16), 'space')  87.5 us
    dot_general x18, matrix products, conv_views(): jnp.einsum('nrcw,oc->nrow', window, weight[row_tap, col_tap], preferred_e...  50.9 us
    all_gather x1, waiting for transfers between devices, gather_channels(): return lax.all_gather(act, 'chan', axis=2, tiled=True)  24.2 us
    dot_general x9, matrix products, weight_terms(): jnp.einsum('nrow,nrcw->oc', grad_field, window, preferred_element_type=jn...  11.9 us
    unnamed x49, local copies, waits for them, and re-layouts  9.95 us
    all_to_all x1, starting transfers between devices, receive_tiles(): lax.all_to_all(outgoing, 'space', split_axis=0, concat_axis=0, tiled=True)  6.04 us
    reduce_sum x6, other arithmetic, group_sums(): return jnp.sum(grouped, axis=(-2, -1))  5.37 us
  transfers between devices with their start and end apart: 4, of which 3 were waited for; matrix products, arithmetic and copies ran while one was open for 13% of the time, Pallas kernels for 0%

profile of v1, /device:TPU:18, one launch (start us, length us, event | category | flops | bytes accessed | tf_op | source)
XLA Modules:
  0.0 258.4 jit_solution(17546179747258794243)
XLA Ops:
  7.3 2.0 multiply_reduce_fusion.1
  9.3 1.2 convert_element_type.101
  12.6 1.7 select_convert_fusion
  14.6 1.4 reverse_bitcast_fusion
  16.0 24.2 %all-gather.2.cloned.1.call-done = bf16[1,16,640,128]{3,2,1,0:T(8,128)(2,1)} async-done(((bf16[1,16,160,128]{3,2,1,0:T(8,128)(2,1)}), bf16[1,16,640,128]{3,2,1,0:T(8,128)(2,1)}) %all-gather.2.cloned.1.call-update) | async-done | bytes 2621456 | tf_op jit(solution)/shard_map/all_gather | solution.py:74
  40.2 2.8 %fusion.217 = (bf16[1,15,640,128]{3,2,1,0:T(8,128)(2,1)S(1)}, bf16[1,15,640,128]{3,2,1,0:T(8,128)(2,1)S(1)}) fusion(bf16[1,16,640,128]{3,2,1,0:T(8,128)(2,1)} %all-gather.2.cloned.1.call-done), kind=kLoop, calls=%fused_computation.229 | loop fusion | bytes 9830400 | tf_op jit(solution)/shard_map/slice | solution.py:127
  43.2 1.1 copy-done.9
  52.3 1.2 fusion.59
  53.5 1.2 fusion.80
  55.0 1.2 copy-done.11
  56.2 3.2 %fusion.115 = f32[16,128,640]{1,2,0:T(8,128)} fusion(bf16[1,16,160,128]{3,2,1,0:T(8,128)(2,1)S(1)} %pad_select_fusion.3, bf16[3,3,640,160]{2,3,1,0:T(8,128)(2,1)S(1)} %copy-done.11), kind=kOutput, calls=%fused_computation.92 | convolution fusion | flops 419430400 | bytes 6103040 | tf_op jit(solution)/shard_map/nrcw,oc->nrow/dot_general | solution.py:47
  59.5 3.4 %fusion.118 = f32[16,128,640]{1,2,0:T(8,128)} fusion(bf16[1,16,160,128]{3,2,1,0:T(8,128)(2,1)S(1)} %pad_select_fusion.3, bf16[3,3,640,160]{2,3,1,0:T(8,128)(2,1)S(1)} %copy-done.11), kind=kOutput, calls=%fused_computation.94 | convolution fusion | flops 419430400 | bytes 6103040 | tf_op jit(solution)/shard_map/nrcw,oc->nrow/dot_general | solution.py:47
  62.8 3.2 %fusion.144 = f32[16,128,640]{1,2,0:T(8,128)} fusion(bf16[3,3,640,160]{2,3,1,0:T(8,128)(2,1)S(1)} %copy-done.11, bf16[1,15,160,128]{3,2,1,0:T(8,128)(2,1)S(1)} %get-tuple-element.17, pred[16]{0:T(512)(128)(4,1)S(1)} %get-tuple-element.31), kind=kOutput, calls=%fused_computation.115 | convolution fusion | flops 419758080 | bytes 6062592 | tf_op jit(solution)/shard_map/nrcw,oc->nrow/dot_general | solution.py:47
  66.0 3.5 %fusion.121 = f32[16,128,640]{1,2,0:T(8,128)} fusion(bf16[1,16,160,128]{3,2,1,0:T(8,128)(2,1)S(1)} %fusion.80, bf16[3,3,640,160]{2,3,1,0:T(8,128)(2,1)S(1)} %copy-done.11), kind=kOutput, calls=%fused_computation.96 | convolution fusion | flops 419430400 | bytes 6103040 | tf_op jit(solution)/shard_map/nrcw,oc->nrow/dot_general | solution.py:47
  69.4 3.3 %fusion.124 = f32[16,128,640]{1,2,0:T(8,128)} fusion(bf16[1,16,160,128]{3,2,1,0:T(8,128)(2,1)S(1)} %fusion.80, bf16[3,3,640,160]{2,3,1,0:T(8,128)(2,1)S(1)} %copy-done.11), kind=kOutput, calls=%fused_computation.98 | convolution fusion | flops 419430400 | bytes 6103040 | tf_op jit(solution)/shard_map/nrcw,oc->nrow/dot_general | solution.py:47
  72.8 3.1 %fusion.142 = f32[16,128,640]{1,2,0:T(8,128)} fusion(bf16[1,16,160,128]{3,2,1,0:T(8,128)(2,1)S(1)} %fusion.80, bf16[3,3,640,160]{2,3,1,0:T(8,128)(2,1)S(1)} %copy-done.11), kind=kOutput, calls=%fused_computation.113 | convolution fusion | flops 419430400 | bytes 6103040 | tf_op jit(solution)/shard_map/nrcw,oc->nrow/dot_general | solution.py:47
  76.0 3.2 %fusion.131 = f32[16,128,640]{1,2,0:T(8,128)} fusion(bf16[3,3,640,160]{2,3,1,0:T(8,128)(2,1)S(1)} %copy-done.11, bf16[1,15,160,128]{3,2,1,0:T(8,128)(2,1)S(1)} %get-tuple-element.18, pred[16]{0:T(512)(128)(4,1)S(1)} %get-tuple-element.32), kind=kOutput, calls=%fused_computation.102 | convolution fusion | flops 419758080 | bytes 6062592 | tf_op jit(solution)/shard_map/nrcw,oc->nrow/dot_general | solution.py:47
  79.3 3.3 %fusion.127 = f32[16,128,640]{1,2,0:T(8,128)} fusion(bf16[1,16,160,128]{3,2,1,0:T(8,128)(2,1)S(1)} %pad_select_fusion.2, bf16[3,3,640,160]{2,3,1,0:T(8,128)(2,1)S(1)} %copy-done.11), kind=kOutput, calls=%fused_computation.100 | convolution fusion | flops 419430400 | bytes 6103040 | tf_op jit(solution)/shard_map/nrcw,oc->nrow/dot_general | solution.py:47
  82.6 16.0 %fusion.1 = bf16[1,16,640,128]{3,2,1,0:T(8,128)(2,1)} fusion(f32[16,128,640]{1,2,0:T(8,128)} %fusion.131, f32[16,128,640]{1,2,0:T(8,128)} %fusion.127, f32[16,128,640]{1,2,0:T(8,128)} %fusion.124, f32[16,128,640]{1,2,0:T(8,128)} %fusion.142, f32[16,128,640]{1,2,0:T(8,128)} %fusion.121, f32[16,128,640]{1,2,0:T(8,128)} %fusion.118, ...), kind=kOutput, calls=%fused_computation.9 | convolution fusion | flops 431226880 | bytes 45424640 | tf_op jit(solution)/shard_map/nrcw,oc->nrow/dot_general | solution.py:47
  115.4 3.0 %fusion.84 = f32[1,160,640]{2,1,0:T(8,128)S(1)} fusion(bf16[1,16,640,128]{3,2,1,0:T(8,128)(2,1)} %copy-done.1, bf16[1,16,160,128]{3,2,1,0:T(8,128)(2,1)S(1)} %fusion.80), kind=kOutput, calls=%fused_computation.74 | convolution fusion | flops 419430400 | bytes 3686400 | tf_op jit(solution)/shard_map/nrow,nrcw->oc/dot_general | solution.py:67
  118.5 1.2 fusion.87
  121.3 1.1 fusion.90
  122.5 1.2 fusion.93
  125.4 1.2 fusion.96
  126.5 1.2 fusion.99
  129.4 1.6 fusion
  131.0 2.4 reduce-scatter.2.cloned.1.call-done
  133.4 3.0 %fusion.216 = (f32[16,160]{1,0:T(8,128)S(1)}, f32[16,160]{1,0:T(8,128)S(1)}, f32[1,16,160,128]{3,2,1,0:T(8,128)S(1)}) fusion(f32[16,160]{1,0:T(8,128)S(1)} %mul.162, f32[16,160]{1,0:T(8,128)S(1)} %sub.65, f32[160]{0:T(256)S(1)} %copy-done.16, f32[160]{0:T(256)S(1)} %copy-done.17, bf16[1,16,160,128]{3,2,1,0:T(8,128)(2,1)} %reduce-scatter.2.cloned.1.call-done, ...), kind=kLoop, calls=%fused_computation.228 | loop fusion | flops 5565440 | bytes 3319040 | tf_op jit(solution)/shard_map/reduce_sum | solution.py:30
  138.0 1.7 multiply_convert_fusion
  144.8 6.0 %all-to-all-start = ((bf16[8,2,160,128]{3,2,1,0:T(8,128)(2,1)}), bf16[8,2,160,128]{3,2,1,0:T(8,128)(2,1)S(1)}, u32[]{:S(2)}, u32[]{:S(2)}) async-start(bf16[8,2,160,128]{3,2,1,0:T(8,128)(2,1)} %dynamic-slice_dynamic-update-slice_fusion), calls=%async_computation.1 | async-start | bytes 1310720 | tf_op jit(solution)/shard_map/all_to_all | solution.py:84
  159.9 87.5 %all-reduce.12.cloned.1.call-done = bf16[3,3,160,640]{3,2,1,0:T(8,128)(2,1)} async-done(((bf16[3,3,160,640]{3,2,1,0:T(8,128)(2,1)}), bf16[3,3,160,640]{3,2,1,0:T(8,128)(2,1)}) %all-reduce.12.cloned.1.call-update) | async-done | bytes 1843216 | tf_op jit(solution)/shard_map/psum | solution.py:155
  247.4 3.6 %convert_element_type.114 = f32[3,3,160,640]{3,2,1,0:T(8,128)} convert(bf16[3,3,160,640]{3,2,1,0:T(8,128)(2,1)} %all-reduce.12.cloned.1.call-done) | non-fusion elementwise | flops 921600 | bytes 5529600 | tf_op jit(solution)/shard_map/convert_element_type | solution.py:155
  (114 shorter events, 26.1 us)
Async XLA Ops:
  7.2 3.3 %copy-start.14 = (s32[8,8]{1,0:T(8,128)S(1)}, s32[8,8]{1,0:T(8,128)}, u32[]{:S(2)}) copy-start(s32[8,8]{1,0:T(8,128)} %param.14) | copy-start | bytes 772
  7.2 3.4 %copy-start.15 = (s32[8,8]{1,0:T(8,128)S(1)}, s32[8,8]{1,0:T(8,128)}, u32[]{:S(2)}) copy-start(s32[8,8]{1,0:T(8,128)} %param.15) | copy-start | bytes 772
  7.2 33.0 %all-gather.2.cloned.1.call-start = ((), (), s32[]{:S(2)}) async-start(), calls=%async_computation.2 | async-start | bytes 3276800 | tf_op jit(solution)/shard_map/all_gather | solution.py:74
  7.2 5.4 %copy-start.16 = (f32[160]{0:T(256)S(1)}, f32[160]{0:T(256)}, u32[]{:S(2)}) copy-start(f32[160]{0:T(256)} %param.12) | copy-start | bytes 1924
  7.2 5.4 %copy-start.17 = (f32[160]{0:T(256)S(1)}, f32[160]{0:T(256)}, u32[]{:S(2)}) copy-start(f32[160]{0:T(256)} %param.11) | copy-start | bytes 1924
  10.5 3.9 %copy-start.3 = (f32[8,2,160,128]{3,2,1,0:T(8,128)}, f32[8,2,160,128]{3,2,1,0:T(8,128)S(1)}, u32[]{:S(2)}) copy-start(f32[8,2,160,128]{3,2,1,0:T(8,128)S(1)} %convert_element_type.101) | copy-start | bytes 3932164
  10.6 3.8 %copy-start.20 = (s32[16]{0:T(128)S(1)}, s32[16]{0:T(128)}, u32[]{:S(2)}) copy-start(s32[16]{0:T(128)} %param.17) | copy-start | bytes 196
  11.0 3.6 %copy-start.12 = (bf16[3,3,160,640]{3,2,1,0:T(8,128)(2,1)S(1)}, bf16[3,3,160,640]{3,2,1,0:T(8,128)(2,1)}, u32[]{:S(2)}) copy-start(bf16[3,3,160,640]{3,2,1,0:T(8,128)(2,1)} %param.13) | copy-start | bytes 5529604
  14.4 119.1 %reduce-scatter.2.cloned.1.call-start = ((), (), s32[]{:S(2)}) async-start(), calls=%async_computation.3 | async-start | bytes 3276800 | tf_op jit(solution)/shard_map/reduce_scatter | solution.py:78
  42.9 1.4 copy-start.9
  43.0 2.4 copy-start.7
  44.4 6.1 %copy-start.1 = (bf16[1,16,640,128]{3,2,1,0:T(8,128)(2,1)}, bf16[1,16,640,128]{3,2,1,0:T(8,128)(2,1)S(1)}, u32[]{:S(2)}) copy-start(bf16[1,16,640,128]{3,2,1,0:T(8,128)(2,1)S(1)} %pad_select_fusion.1) | copy-start | bytes 7864324
  45.4 8.1 %copy-start.5 = (bf16[1,16,640,128]{3,2,1,0:T(8,128)(2,1)}, bf16[1,16,640,128]{3,2,1,0:T(8,128)(2,1)S(1)}, u32[]{:S(2)}) copy-start(bf16[1,16,640,128]{3,2,1,0:T(8,128)(2,1)S(1)} %pad_select_fusion) | copy-start | bytes 7864324
  46.1 1.6 copy-start.13
  47.7 1.7 copy-start
  52.3 1.2 copy-start.19
  54.7 1.5 copy-start.11
  98.6 148.8 %all-reduce.12.cloned.1.call-start = ((), (), s32[]{:S(2)}) async-start(), calls=%async_computation.4 | async-start | bytes 3686400 | tf_op jit(solution)/shard_map/psum | solution.py:155
  115.4 3.1 %copy-start.2 = (bf16[1,16,640,128]{3,2,1,0:T(8,128)(2,1)S(1)}, bf16[1,16,640,128]{3,2,1,0:T(8,128)(2,1)}, u32[]{:S(2)}) copy-start(bf16[1,16,640,128]{3,2,1,0:T(8,128)(2,1)} %copy-done.1) | copy-start | bytes 7864324
  118.4 1.7 copy-start.10
  123.6 1.7 copy-start.6
  126.5 1.7 copy-start.8
  131.0 2.4 copy-start.4
  139.7 11.2 %copy-start.18 = (s32[8,8]{1,0:T(8,128)S(1)}, s32[8,8]{1,0:T(8,128)}, u32[]{:S(2)}) copy-start(s32[8,8]{1,0:T(8,128)} %param.16) | copy-start | bytes 772
  144.8 106.3 %all-to-all-start = ((bf16[8,2,160,128]{3,2,1,0:T(8,128)(2,1)}), bf16[8,2,160,128]{3,2,1,0:T(8,128)(2,1)S(1)}, u32[]{:S(2)}, u32[]{:S(2)}) async-start(bf16[8,2,160,128]{3,2,1,0:T(8,128)(2,1)} %dynamic-slice_dynamic-update-slice_fusion), calls=%async_computation.1 | async-start | bytes 1310720 | tf_op jit(solution)/shard_map/all_to_all | solution.py:84
Sparse Core Ops, SparseCore 0:
  14.5 25.6 all-gather.1
  98.7 34.6 reduce-scatter.1
  137.5 109.8 all-reduce.11

commit v2 on v1

v2 whole, which is shorter than its diff:
```python
import functools
import math

import jax
import jax.numpy as jnp
from jax import lax
from jax.experimental import pallas as pl
from jax.experimental.pallas import tpu as pltpu
from jax.sharding import PartitionSpec as P

GROUPS = 32
EPS = 1e-05
HIGH = lax.Precision.HIGHEST
F32, BF16 = jnp.float32, jnp.bfloat16
MESH = pl.DeviceIdType.MESH
CHUNKS = 4


def loss_weights(timesteps):
    phase = (timesteps.astype(F32) / 1000.0 + 0.008) / 1.008 * (math.pi / 2.0)
    alpha_bar = jnp.cos(phase) ** 2
    return jnp.minimum(1.0, 5.0 * (1.0 - alpha_bar) / alpha_bar)


def kernel(
    n, grad_scale, ti, to, ts, lw, gb, lat, tgt, w, xo, wo,
    act, mybuf, agbuf, act_t, pre_w, field, w_t, wbuf, wy, ybuf, zsend, zbuf, own, gzbuf, gybuf,
    part, sib_far, sib_near, x_send, x_recv, stat, ngrad, xg, outg, inb,
    ag_send, ag_recv, y_send, y_recv, z_send, z_recv, gz_send, gz_recv,
    gy_send, gy_recv, a_send, a_recv, r_send, r_recv,
):
    slots, trows, loc, cols = lat.shape
    nrow = slots * trows
    rows9, chans = w.shape
    tiles_dev = xo.shape[0]
    group = chans // GROUPS
    nz = n // 2
    piece = wbuf.shape[1]
    half = nz * piece
    padded = 2 * half
    span = nrow * cols // CHUNKS
    me = lax.axis_index("space")
    ch = lax.axis_index("chan")
    my_y, my_z = lax.rem(me, 2), me // 2
    y_dev = my_z * 2 + 1 - my_y
    core, my_x = lax.rem(ch, 2), ch // 2
    sib = my_x * 2 + 1 - core
    xn = (1 - my_x) * 2 + core
    diag = (1 - my_x) * 2 + 1 - core

    def rc(src, dst, ss, rs, space=None, chan=None):
        return pltpu.make_async_remote_copy(
            src_ref=src, dst_ref=dst, send_sem=ss, recv_sem=rs,
            device_id={
                "space": me if space is None else space,
                "chan": ch if chan is None else chan,
            },
            device_id_type=MESH,
        )

    barrier = pltpu.get_barrier_semaphore()
    for k in range(1, n):
        pl.semaphore_signal(
            barrier, inc=1, device_id={"space": lax.rem(me + k, n), "chan": ch},
            device_id_type=MESH,
        )
    for other in (sib, xn):
        pl.semaphore_signal(
            barrier, inc=1, device_id={"space": me, "chan": other}, device_id_type=MESH
        )

    image = [ti[me, j] for j in range(slots)]
    first = image[0]
    used_i = [(v >= 0).astype(jnp.int32) for v in image]
    is_b = [jnp.where((v >= 0) & (v != first), 1, 0) for v in image]
    used = [u.astype(F32) for u in used_i]
    mask_b = [b.astype(F32) for b in is_b]
    mask_a = [u - b for u, b in zip(used, mask_b)]
    same = [
        jnp.where((image[j] >= 0) & (image[j] == image[j + 1]), 1.0, 0.0).astype(F32)
        for j in range(slots - 1)
    ]
    per_slot = float(trows * cols * group)
    count_a = jnp.maximum(sum(mask_a), 1.0) * per_slot
    count_b = jnp.maximum(sum(mask_b), 1.0) * per_slot
    loss = [lw[jnp.maximum(v, 0)] * u for v, u in zip(image, used)]
    up = [(1.0 if r % trows else (same[r // trows - 1] if r else 0.0)) for r in range(nrow)]
    up = [u * used[r // trows] for r, u in enumerate(up)]
    down = [
        (1.0 if r % trows < trows - 1 else (same[r // trows] if r < nrow - 1 else 0.0))
        for r in range(nrow)
    ]
    down = [u * used[r // trows] for r, u in enumerate(down)]

    gain, bias = gb[0], gb[1]
    chan_row = lax.broadcasted_iota(jnp.int32, (loc, loc), 0) // group
    chan_col = lax.broadcasted_iota(jnp.int32, (loc, loc), 1) // group
    same_group = jnp.where(chan_row == chan_col, 1.0, 0.0).astype(F32)
    lane = lax.broadcasted_iota(jnp.int32, (loc, cols), 1)

    def group_total(values):
        summed = jnp.sum(values, axis=1, keepdims=True)
        wide = jnp.broadcast_to(summed, (loc, cols))
        return jnp.dot(same_group, wide, precision=HIGH, preferred_element_type=F32)

    sums = [jnp.zeros((loc, cols), F32) for _ in range(4)]
    for j in range(slots):
        x0 = lat[j, 0].astype(F32)
        total, square = x0, x0 * x0
        for t in range(1, trows):
            xt = lat[j, t].astype(F32)
            total, square = total + xt, square + xt * xt
        sums = [
            sums[0] + mask_a[j] * total, sums[1] + mask_a[j] * square,
            sums[2] + mask_b[j] * total, sums[3] + mask_b[j] * square,
        ]
    for i, count in enumerate((count_a, count_b)):
        mean = group_total(sums[2 * i]) / count
        var = group_total(sums[2 * i + 1]) / count - mean * mean
        stat[i, 0] = mean
        stat[i, 1] = lax.rsqrt(var + EPS)

    def pre_of(r):
        j = r // trows
        mean, rstd = stat[is_b[j], 0], stat[is_b[j], 1]
        normed = (lat[j, r % trows].astype(F32) - mean) * rstd
        return normed, normed * gain + bias, rstd

    mine = pl.ds(pl.multiple_of(ch * loc, 16), loc)

    def ag_copy(kind, c):
        source = (mybuf.at[c], mybuf.at[c], agbuf.at[1, c])[kind]
        return rc(
            source, agbuf.at[kind, c], ag_send.at[kind, c], ag_recv.at[kind, c],
            chan=(sib, xn, sib)[kind],
        )

    pl.semaphore_wait(barrier, n + 1)
    for c in range(CHUNKS):
        for r in range(c * nrow // CHUNKS, (c + 1) * nrow // CHUNKS):
            _, pre, _ = pre_of(r)
            value = pre * jax.nn.sigmoid(pre) * used[r // trows]
            mybuf[c, :, pl.ds(r * cols - c * span, cols)] = value.astype(BF16)
        ag_copy(1, c).start()
        ag_copy(0, c).start()

    pad = padded - rows9
    full_blocks = rows9 // 128
    for i in range(full_blocks):
        w_t[:, pl.ds(i * 128, 128)] = w[pl.ds(i * 128, 128), :].T
    rest = rows9 - full_blocks * 128
    if rest:
        tail = jnp.concatenate(
            [w[pl.ds(full_blocks * 128, rest), :], jnp.zeros((128 - rest, chans), BF16)], axis=0
        )
        w_t[:, pl.ds(full_blocks * 128, 128)] = tail.T
        done = (full_blocks + 1) * 128
    else:
        done = rows9
    if done < rows9 + pad:
        w_t[:, pl.ds(done, rows9 + pad - done)] = jnp.zeros((chans, rows9 + pad - done), BF16)
    field[pl.ds(rows9, pad), :] = jnp.zeros((pad, nrow * cols), BF16)
    third = rows9 // 3
    field[pl.ds(0, third), pl.ds((nrow - 1) * cols, cols)] = jnp.zeros((third, cols), BF16)
    field[pl.ds(2 * third, third), pl.ds(0, cols)] = jnp.zeros((third, cols), BF16)

    def from_left(v):
        return jnp.where(lane == 0, 0.0, pltpu.roll(v, 1, 1))

    def from_right(v):
        return jnp.where(lane == cols - 1, 0.0, pltpu.roll(v, cols - 1, 1))

    def taps(row_tap, col_tap, r):
        return pre_w[pl.ds((row_tap * 3 + col_tap) * loc, loc), pl.ds(r * cols, cols)]

    def out_row(r):
        j = r // trows
        total = []
        for col_tap in range(3):
            value = taps(1, col_tap, r)
            if r > 0:
                value = value + up[r] * taps(0, col_tap, r - 1)
            if r < nrow - 1:
                value = value + down[r] * taps(2, col_tap, r + 1)
            total.append(value)
        pred = total[1] + from_left(total[0]) + from_right(total[2])
        grad = loss[j] * (pred - tgt[j, r % trows].astype(F32))
        grad = grad.astype(BF16).astype(F32)
        for col_tap, moved in enumerate((from_right(grad), grad, from_left(grad))):
            def put(row_tap, row, value):
                field[
                    pl.ds((row_tap * 3 + col_tap) * loc, loc), pl.ds(row * cols, cols)
                ] = value.astype(BF16)
            put(1, r, moved)
            if r > 0:
                put(0, r - 1, up[r] * moved)
            if r < nrow - 1:
                put(2, r + 1, down[r] * moved)

    rows_chunk = nrow // CHUNKS
    for c in range(CHUNKS):
        ag_copy(1, c).wait_recv()
        ag_copy(2, c).start()
        ag_copy(0, c).wait_recv()
        ag_copy(2, c).wait_recv()
        here = pl.ds(c * span, span)
        act[mine, here] = mybuf[c]
        for kind, index in enumerate((sib, xn, diag)):
            act[pl.ds(pl.multiple_of(index * loc, 16), loc), here] = agbuf[kind, c]
        for i in range(3):
            pre_w[pl.ds(i * third, third), here] = jnp.dot(
                w[pl.ds(i * third, third), :], act[:, here], preferred_element_type=F32
            )
        act_t[here, :] = act[:, here].T
        low = max(0, c * rows_chunk - 1)
        high = nrow if c == CHUNKS - 1 else (c + 1) * rows_chunk - 1
        for r in range(low, high):
            out_row(r)

    def weight_part(y):
        start = pl.multiple_of(y * half, 16)
        total = jnp.dot(field[pl.ds(start, half), :], act_t[...], preferred_element_type=F32)
        return (total * grad_scale).astype(BF16).reshape(nz, piece, chans)

    def y_copy(k):
        return rc(
            wy.at[lax.rem(my_z + k, nz)], ybuf.at[k], y_send.at[k], y_recv.at[k], space=y_dev
        )

    order = list(range(1, nz)) + [0]
    wy[...] = weight_part(1 - my_y)
    for k in order:
        y_copy(k).start()
    wbuf[...] = weight_part(my_y)

    for c in range(CHUNKS):
        here = pl.ds(c * span, span)
        part[:, here] = jnp.dot(
            w_t[...], field[:, here], preferred_element_type=F32
        ).astype(BF16)

    def block(index):
        return pl.ds(pl.multiple_of(index * loc, 16), loc)

    far_copy = rc(part.at[block(diag)], sib_far, r_send.at[0], r_recv.at[0], chan=sib)
    near_copy = rc(part.at[block(sib)], sib_near, r_send.at[1], r_recv.at[1], chan=sib)
    x_copy = rc(x_send, x_recv, r_send.at[2], r_recv.at[2], chan=xn)
    far_copy.start()
    near_copy.start()
    far_copy.wait_recv()
    x_send[...] = (part[block(xn), :].astype(F32) + sib_far[...].astype(F32)).astype(BF16)
    x_copy.start()

    def z_copy(k):
        z = lax.rem(my_z + k, nz)
        return rc(
            zsend.at[k], zbuf.at[k], z_send.at[k], z_recv.at[k], space=z * 2 + my_y
        )

    for k in order:
        y_copy(k).wait_recv()
        z = lax.rem(my_z + k, nz)
        zsend[k] = (wbuf[z].astype(F32) + ybuf[k].astype(F32)).astype(BF16)
        if k:
            z_copy(k).start()

    near_copy.wait_recv()
    x_copy.wait_recv()
    sums = [jnp.zeros((loc, cols), F32) for _ in range(4)]
    for j in range(slots):
        total, second = None, None
        for t in range(trows):
            r = j * trows + t
            at = pl.ds(r * cols, cols)
            grad = (
                part[mine, at].astype(F32) + sib_near[:, at].astype(F32)
            ) + x_recv[:, at].astype(F32)
            normed, pre, _ = pre_of(r)
            s = jax.nn.sigmoid(pre)
            value = grad * (s * (1.0 + pre * (1.0 - s))) * gain
            ngrad[r] = value
            total = value if total is None else total + value
            second = value * normed if second is None else second + value * normed
        sums = [
            sums[0] + mask_a[j] * total, sums[1] + mask_a[j] * second,
            sums[2] + mask_b[j] * total, sums[3] + mask_b[j] * second,
        ]
    for i, count in enumerate((count_a, count_b)):
        stat[i, 2] = group_total(sums[2 * i]) / count
        stat[i, 3] = group_total(sums[2 * i + 1]) / count
    for r in range(nrow):
        j = r // trows
        normed, _, rstd = pre_of(r)
        mean_g, mean_gn = stat[is_b[j], 2], stat[is_b[j], 3]
        xg[j, r % trows] = (rstd * (ngrad[r] - mean_g - normed * mean_gn)).astype(BF16)
    for k in range(n):
        d = lax.rem(me + k, n)
        slot = jnp.int32(0)
        for j in range(slots):
            slot = jnp.where(to[me, j] == d, j, slot)
        if k:
            outg[k] = xg[slot]
        else:
            inb[0] = xg[slot]

    total = zsend[0].astype(F32)
    for k in range(1, nz):
        z_copy(k).wait_recv()
        total = total + zbuf[k].astype(F32)
    own[...] = total.astype(BF16)

    def gz_copy(k):
        z = lax.rem(my_z + k, nz)
        return rc(own, gzbuf.at[k], gz_send.at[k], gz_recv.at[k], space=z * 2 + my_y)

    def gy_copy(k):
        source = gzbuf.at[k] if k else own
        return rc(source, gybuf.at[k], gy_send.at[k], gy_recv.at[k], space=y_dev)

    for k in range(1, nz):
        gz_copy(k).start()
    gy_copy(0).start()

    def a_copy(k):
        return rc(
            outg.at[k], inb.at[k], a_send.at[k], a_recv.at[k], space=lax.rem(me + k, n)
        )

    for k in range(1, n):
        a_copy(k).start()

    def put_piece(y, k, value):
        z = lax.rem(my_z - k + nz, nz)
        wo[pl.ds(pl.multiple_of((y * nz + z) * piece, 16), piece), :] = value

    put_piece(my_y, 0, own[...])
    for k in range(1, nz):
        gz_copy(k).wait_recv()
        gy_copy(k).start()
        put_piece(my_y, k, gzbuf[k])

    def find(step, found):
        s, j = step // slots, lax.rem(step, slots)
        owner, place = to[s, j], ts[s, j]
        return tuple(
            jnp.where((owner == me) & (place == t), s, found[t]) for t in range(tiles_dev)
        )

    found = lax.fori_loop(0, n * slots, find, tuple(jnp.int32(0) for _ in range(tiles_dev)))
    for k in range(1, n):
        a_copy(k).wait_recv()
    for t in range(tiles_dev):
        xo[t] = inb[lax.rem(me - found[t] + n, n)]
    for k in range(nz):
        gy_copy(k).wait_recv()
        put_piece(1 - my_y, k, gybuf[k])

    for c in range(CHUNKS):
        for kind in range(3):
            ag_copy(kind, c).wait_send()
    for z in range(nz):
        y_copy(z).wait_send()
        gy_copy(z).wait_send()
    for k in range(1, nz):
        z_copy(k).wait_send()
        gz_copy(k).wait_send()
    for k in range(1, n):
        a_copy(k).wait_send()
    for copy in (far_copy, near_copy, x_copy):
        copy.wait_send()


def local(
    latents, targets, norm_gain, norm_bias, conv_weight, tile_image, tile_owner, tile_slot,
    timesteps,
):
    n = lax.axis_size("space")
    slots, trows, loc, cols = latents.shape
    chans = conv_weight.shape[3]
    tiles_dev = slots // 2
    rows9 = 9 * loc
    wide = slots * trows * cols
    step = math.lcm(16 * n, 256)
    padded = -(-rows9 // step) * step
    nz = n // 2
    piece = padded // n
    grad_scale = 1.0 / math.sqrt(n * tiles_dev * trows * cols)
    gb = jnp.broadcast_to(
        jnp.stack([norm_gain, norm_bias])[:, :, None], (2, loc, cols)
    )
    smem = pl.BlockSpec(memory_space=pltpu.SMEM)
    vmem = pl.BlockSpec(memory_space=pltpu.VMEM)
    dma = pltpu.SemaphoreType.DMA
    x_grad, weight = pl.pallas_call(
        functools.partial(kernel, n, grad_scale),
        out_shape=(
            jax.ShapeDtypeStruct((tiles_dev, trows, loc, cols), BF16),
            jax.ShapeDtypeStruct((padded, chans), BF16),
        ),
        in_specs=[smem] * 4 + [vmem] * 4,
        out_specs=(vmem, vmem),
        scratch_shapes=[
            pltpu.VMEM((chans, wide), BF16),
            pltpu.VMEM((CHUNKS, loc, wide // CHUNKS), BF16),
            pltpu.VMEM((3, CHUNKS, loc, wide // CHUNKS), BF16),
            pltpu.VMEM((wide, chans), BF16),
            pltpu.VMEM((rows9, wide), F32),
            pltpu.VMEM((padded, wide), BF16),
            pltpu.VMEM((chans, padded), BF16),
            *[pltpu.VMEM((nz, piece, chans), BF16)] * 5,
            pltpu.VMEM((piece, chans), BF16),
            *[pltpu.VMEM((nz, piece, chans), BF16)] * 2,
            pltpu.VMEM((chans, wide), BF16),
            pltpu.VMEM((loc, wide), BF16),
            pltpu.VMEM((loc, wide), BF16),
            pltpu.VMEM((loc, wide), BF16),
            pltpu.VMEM((loc, wide), BF16),
            pltpu.VMEM((2, 4, loc, cols), F32),
            pltpu.VMEM((slots * trows, loc, cols), F32),
            pltpu.VMEM((slots, trows, loc, cols), BF16),
            pltpu.VMEM((n, trows, loc, cols), BF16),
            pltpu.VMEM((n, trows, loc, cols), BF16),
            dma((3, CHUNKS)), dma((3, CHUNKS)),
            dma((nz,)), dma((nz,)), dma((nz,)), dma((nz,)), dma((nz,)), dma((nz,)),
            dma((nz,)), dma((nz,)), dma((n,)), dma((n,)), dma((3,)), dma((3,)),
        ],
        compiler_params=pltpu.CompilerParams(
            collective_id=0, has_side_effects=True, vmem_limit_bytes=62 * 1024 * 1024
        ),
    )(
        tile_image, tile_owner, tile_slot, loss_weights(timesteps), gb, latents, targets,
        conv_weight.reshape(rows9, chans),
    )
    return x_grad, weight[:rows9].astype(F32).reshape(conv_weight.shape)


def solution(mesh):
    in_specs = (
        P("space", None, "chan", None),
        P("space", None, "chan", None),
        P("chan"),
        P("chan"),
        P(None, None, "chan", None),
        P(),
        P(),
        P(),
        P(),
    )
    out_specs = (P("space", None, "chan", None), P(None, None, "chan", None))
    return jax.shard_map(local, mesh=mesh, in_specs=in_specs, out_specs=out_specs, check_vma=False)
```

time: 261 us -> 114 us (0.44); the launches traced: 258 us -> 114 us
  waiting for transfers between devices: 114 us -> 0 us
  Pallas kernels: 0 us -> 106 us
  matrix products: 64.6 us -> 0 us
  between operations: 37.3 us -> 0.65 us
  other arithmetic: 18.6 us -> 4.06 us
  local copies, waits for them, and re-layouts: 17.6 us -> 3.17 us
  starting transfers between devices: 6.16 us -> 0 us
    pallas_call x0 -> x1, Pallas kernels: none -> 106 us  [local(): pl.pallas_call(functools.partial(kernel, n, grad_scale), out_shape=(jax.S...]
    psum x1 -> x0, waiting for transfers between devices: 87.5 us -> none  [local(): lax.psum((weight_sum * grad_scale).astype(jnp.bfloat16), 'space')]
    dot_general x36 -> x0, matrix products: 64.6 us -> none  [the longest x18 50.9 us: conv_views(): jnp.einsum('nrcw,oc->nrow', window, weight[row_tap, col_tap], preferred_e...]
    all_gather x1 -> x0, waiting for transfers between devices: 24.2 us -> none  [gather_channels(): return lax.all_gather(act, 'chan', axis=2, tiled=True)]
    convert_element_type x5 -> x0, other arithmetic: 9.88 us -> none  [the longest x1 3.63 us: local(): lax.psum((weight_sum * grad_scale).astype(jnp.bfloat16), 'space')]
    unnamed x49 -> x3, local copies, waits for them, and re-layouts: 9.95 us -> 0.73 us
    all_to_all x1 -> x0, starting transfers between devices: 6.04 us -> none  [receive_tiles(): lax.all_to_all(outgoing, 'space', split_axis=0, concat_axis=0, tiled=True)]
    reduce_sum x7 -> x0, other arithmetic: 5.48 us -> none  [the longest x6 5.37 us: group_sums(): return jnp.sum(grouped, axis=(-2, -1))]
  transfers between devices with their start and end apart: 4 -> 0, of which waited for: 3 -> 0; matrix products, arithmetic and copies ran while one was open for 13% -> 0% of each run, Pallas kernels for 0% -> 0%
where the time goes in v2:
time: 114 us
  Pallas kernels  106 us (93%)
  other arithmetic  4.06 us (4%)
  local copies, waits for them, and re-layouts  3.17 us (3%)
    pallas_call x1, Pallas kernels, local(): pl.pallas_call(functools.partial(kernel, n, grad_scale), out_shape=(jax.S...  106 us

profile of v2, /device:TPU:18, one launch (start us, length us, event | category | flops | bytes accessed | tf_op | source)
XLA Modules:
  0.0 114.3 jit_solution(922103837759523578)
XLA Ops:
  0.6 1.2 %fusion.lw = f32[16]{0:T(128)} fusion(s32[16]{0:T(128)} %param.17), kind=kLoop, calls=%fused_computation.2 | loop fusion | flops 144 | bytes 128 | tf_op jit(solution)/shard_map/min | solution.py:22
  1.9 0.7 pad_maximum_fusion
  2.6 0.8 broadcast_in_dim.2.gb
  3.3 106.4 %shard_map.104 = (bf16[4,2,160,128]{3,2,1,0:T(8,128)(2,1)}, bf16[1536,640]{1,0:T(8,128)(2,1)}) custom-call(s32[8,8]{1,0:T(8,128)} %ti.1, s32[8,8]{1,0:T(8,128)} %to.1, s32[8,8]{1,0:T(8,128)} %ts.1, f32[16]{0:T(128)} %fusion.lw, f32[2,160,128]{2,1,0:T(8,128)} %broadcast_in_dim.2.gb, bf16[8,2,160,128]{3,2,1,0:T(8,128)(2,1)} %lat.1, ...), custom_call_target="tpu_custom_call" | custom-call | tf_op jit(solution)/shard_map/pallas_call | solution.py:394
  109.7 1.7 %slice.3 = bf16[1440,640]{1,0:T(8,128)(2,1)S(1)} slice(bf16[1536,640]{1,0:T(8,128)(2,1)} %get-tuple-element.5), slice={[0:1440], [0:640]} | slice | bytes 3686400 | tf_op jit(solution)/shard_map/slice | solution.py:434
  111.4 0.0 copy-start
  111.4 2.1 %convert.1 = f32[3,3,160,640]{3,2,1,0:T(8,128)} convert(bf16[3,3,160,640]{3,2,1,0:T(8,128)(2,1)S(1)} %bitcast.5) | non-fusion elementwise | flops 921600 | bytes 5529600 | tf_op jit(solution)/shard_map/reshape | solution.py:434
  113.5 0.0 copy-done
  113.5 0.7 copy.12
Async XLA Ops:
  111.4 2.1 %copy-start = (bf16[4,2,160,128]{3,2,1,0:T(8,128)(2,1)S(1)}, bf16[4,2,160,128]{3,2,1,0:T(8,128)(2,1)}, u32[]{:S(2)}) copy-start(bf16[4,2,160,128]{3,2,1,0:T(8,128)(2,1)} %get-tuple-element.8) | copy-start | bytes 983044

commit v3 on v2

--- a/solution.py
+++ b/solution.py
@@ -24,7 +24,7 @@
 
 def kernel(
     n, grad_scale, ti, to, ts, lw, gb, lat, tgt, w, xo, wo,
-    act, mybuf, agbuf, act_t, pre_w, field, w_t, wbuf, wy, ybuf, zsend, zbuf, own, gzbuf, gybuf,
+    act, mybuf, agbuf, act_t, pre_w, field, w_t, wbuf, wy, ybuf, zsend, zbuf, own, gzbuf, gybuf, res,
     part, sib_far, sib_near, x_send, x_recv, stat, ngrad, xg, outg, inb,
     ag_send, ag_recv, y_send, y_recv, z_send, z_recv, gz_send, gz_recv,
     gy_send, gy_recv, a_send, a_recv, r_send, r_recv,
@@ -303,6 +303,14 @@
         else:
             inb[0] = xg[slot]
 
+    def a_copy(k):
+        return rc(
+            outg.at[k], inb.at[k], a_send.at[k], a_recv.at[k], space=lax.rem(me + k, n)
+        )
+
+    for k in range(1, n):
+        a_copy(k).start()
+
     total = zsend[0].astype(F32)
     for k in range(1, nz):
         z_copy(k).wait_recv()
@@ -321,17 +329,9 @@
         gz_copy(k).start()
     gy_copy(0).start()
 
-    def a_copy(k):
-        return rc(
-            outg.at[k], inb.at[k], a_send.at[k], a_recv.at[k], space=lax.rem(me + k, n)
-        )
-
-    for k in range(1, n):
-        a_copy(k).start()
-
     def put_piece(y, k, value):
         z = lax.rem(my_z - k + nz, nz)
-        wo[pl.ds(pl.multiple_of((y * nz + z) * piece, 16), piece), :] = value
+        res[pl.ds(pl.multiple_of((y * nz + z) * piece, 16), piece), :] = value
 
     put_piece(my_y, 0, own[...])
     for k in range(1, nz):
@@ -354,6 +354,7 @@
     for k in range(nz):
         gy_copy(k).wait_recv()
         put_piece(1 - my_y, k, gybuf[k])
+    wo[...] = res[pl.ds(0, rows9), :]
 
     for c in range(CHUNKS):
         for kind in range(3):
@@ -395,7 +396,7 @@
         functools.partial(kernel, n, grad_scale),
         out_shape=(
             jax.ShapeDtypeStruct((tiles_dev, trows, loc, cols), BF16),
-            jax.ShapeDtypeStruct((padded, chans), BF16),
+            jax.ShapeDtypeStruct((rows9, chans), BF16),
         ),
         in_specs=[smem] * 4 + [vmem] * 4,
         out_specs=(vmem, vmem),
@@ -410,6 +411,7 @@
             *[pltpu.VMEM((nz, piece, chans), BF16)] * 5,
             pltpu.VMEM((piece, chans), BF16),
             *[pltpu.VMEM((nz, piece, chans), BF16)] * 2,
+            pltpu.VMEM((padded, chans), BF16),
             pltpu.VMEM((chans, wide), BF16),
             pltpu.VMEM((loc, wide), BF16),
             pltpu.VMEM((loc, wide), BF16),
@@ -431,7 +433,7 @@
         tile_image, tile_owner, tile_slot, loss_weights(timesteps), gb, latents, targets,
         conv_weight.reshape(rows9, chans),
     )
-    return x_grad, weight[:rows9].astype(F32).reshape(conv_weight.shape)
+    return x_grad, weight.astype(F32).reshape(conv_weight.shape)
 
 
 def solution(mesh):

time: 114 us -> 118 us (1.035); the launches traced: 114 us -> 117 us
  Pallas kernels: 106 us -> 109 us
  local copies, waits for them, and re-layouts: 3.17 us -> 1.5 us
  other arithmetic: 4.06 us -> 5.61 us
    pallas_call x1, Pallas kernels: 106 us -> 109 us  [local(): pl.pallas_call(functools.partial(kernel, n, grad_scale), out_shape=(jax.S...]
    slice x1 -> x0, local copies, waits for them, and re-layouts: 1.66 us -> none  [local(): return (x_grad, weight[:rows9].astype(F32).reshape(conv_weight.shape))]
    reshape x1, other arithmetic: 2.13 us -> 3.68 us  [local(): return (x_grad, weight.astype(F32).reshape(conv_weight.shape))]
where the time goes in v3:
time: 118 us; the launch traced here: 117 us
  Pallas kernels  109 us (92%)
  other arithmetic  5.61 us (5%)
  local copies, waits for them, and re-layouts  1.5 us (1%)
    pallas_call x1, Pallas kernels, local(): pl.pallas_call(functools.partial(kernel, n, grad_scale), out_shape=(jax.S...  109 us
    reshape x1, other arithmetic, local(): return (x_grad, weight.astype(F32).reshape(conv_weight.shape))  3.68 us

profile of v3, /device:TPU:18, one launch (start us, length us, event | category | flops | bytes accessed | tf_op | source)
XLA Modules:
  0.0 116.7 jit_solution(8531267195923279207)
XLA Ops:
  0.6 1.2 %fusion.lw = f32[16]{0:T(128)} fusion(s32[16]{0:T(128)} %param.17), kind=kLoop, calls=%fused_computation.2 | loop fusion | flops 144 | bytes 128 | tf_op jit(solution)/shard_map/min | solution.py:22
  1.9 0.7 pad_maximum_fusion
  2.6 0.8 broadcast_in_dim.2.gb
  3.3 109.0 %shard_map.104 = (bf16[4,2,160,128]{3,2,1,0:T(8,128)(2,1)}, bf16[1440,640]{1,0:T(8,128)(2,1)}) custom-call(s32[8,8]{1,0:T(8,128)} %ti.1, s32[8,8]{1,0:T(8,128)} %to.1, s32[8,8]{1,0:T(8,128)} %ts.1, f32[16]{0:T(128)} %fusion.lw, f32[2,160,128]{2,1,0:T(8,128)} %broadcast_in_dim.2.gb, bf16[8,2,160,128]{3,2,1,0:T(8,128)(2,1)} %lat.1, ...), custom_call_target="tpu_custom_call" | custom-call | tf_op jit(solution)/shard_map/pallas_call | solution.py:395
  112.3 0.0 copy-start
  112.3 3.7 %convert.1 = f32[3,3,160,640]{3,2,1,0:T(8,128)} convert(bf16[3,3,160,640]{3,2,1,0:T(8,128)(2,1)} %bitcast.6) | non-fusion elementwise | flops 921600 | bytes 5529600 | tf_op jit(solution)/shard_map/reshape | solution.py:436
  116.0 0.0 copy-done
  116.0 0.7 copy.12
Async XLA Ops:
  112.3 3.7 %copy-start = (bf16[4,2,160,128]{3,2,1,0:T(8,128)(2,1)S(1)}, bf16[4,2,160,128]{3,2,1,0:T(8,128)(2,1)}, u32[]{:S(2)}) copy-start(bf16[4,2,160,128]{3,2,1,0:T(8,128)(2,1)} %get-tuple-element.8) | copy-start | bytes 983044
